TPU v7x, 512 devices: a whole 4x8x8 slice. The times are simulated.
512 devices in a mesh: tower: 16 (over x, y_hi), rank: 32 (over y_lo, z, core).
Axes of the slice: x: 4, y: 8 (y_hi: 4, y_lo: 2; y = y_hi * 2 + y_lo), z: 8, core: 2. Of those that a mesh axis runs over, the one named last changes fastest.
Arguments:
- pooled: bfloat16 [2, 8192, 16384], P(None, ('tower', 'rank')), may hold values from -8 to 8
- feature_order: int32 [16, 4], P('tower'), may hold values from 0 to 3, as said below
- cross_weight: bfloat16 [16, 3, 512, 512], P('tower'), may hold values from -0.25 to 0.25
- cross_bias: float32 [16, 3, 512], P('tower'), may hold values from -3 to 3
- compress_weight: bfloat16 [16, 128, 512], P('tower'), may hold values from -0.25 to 0.25
- norm_gain: float32 [16, 128], P('tower'), may hold values from 0.1 to 1.9
- mlp_weight: bfloat16 [4096, 2048], P(('tower', 'rank')), may hold values from -0.125 to 0.125
- mlp_bias: bfloat16 [4096], P(('tower', 'rank')), may hold values from -3 to 3
- out_weight: bfloat16 [4096], P(('tower', 'rank')), may hold values from -0.09375 to 0.09375
Outputs:
- logits: float32 [2, 32, 512], P(None, 'rank', 'tower')
Inputs may be any that keep to these rules, and one draw needn't show every extreme that they name: `feature_order`: each row is an ordering of 0 to 3.
All inputs are finite; a program needn't handle non-finite values.
Results may differ from a plain program's by a relative error of at most 0.0076.
Values may be sent and summed in bfloat16 or wider, within the bound.
No kernel may reach another device: no remote copies, remote signals or barrier semaphores. Data moves between devices by JAX's collectives and lax.ppermute only.
A program may use at most 64 MiB of HBM per device.

v0:
```python
import math
import jax
import jax.numpy as jnp
from jax import lax
from jax.sharding import PartitionSpec as P

E = 128
CD = 128
epsilon = 1e-06


def side_by_side(arrays, axis, dim, along):
    widths = [math.prod(a.shape[along:]) for a in arrays]
    both = jnp.concatenate(
        [a.reshape(*a.shape[:along], w) for a, w in zip(arrays, widths)], axis=along
    )
    whole = lax.all_gather(both, axis, axis=dim, tiled=True)
    parts = jnp.split(whole, [sum(widths[:k]) for k in range(1, len(widths))], axis=along)
    return tuple((b.reshape(*whole.shape[:along], *a.shape[along:]) for a, b in zip(arrays, parts)))


def in_blocks(x, dim, devices):
    shape = x.shape
    parts = x.reshape(*shape[:dim], devices, shape[dim] // devices, *shape[dim + 1 :])
    return jnp.moveaxis(parts, dim, 0)


def summed_on_arrival(x, axis, dim):
    parts = in_blocks(x, dim, lax.axis_size(axis))
    arrived = lax.all_to_all(parts, axis, split_axis=0, concat_axis=0, tiled=True)
    return arrived.sum(axis=0)


def tower_block(first, weights, biases, compress, gain):
    first_f = first.astype(jnp.float32)
    current = first
    for layer in range(weights.shape[0]):
        product = (
            jnp.dot(weights[layer], current, preferred_element_type=jnp.float32)
            + biases[layer][:, None]
        )
        current = (first_f * product + current.astype(jnp.float32)).astype(jnp.bfloat16)
    squeezed = jnp.dot(compress, current, preferred_element_type=jnp.float32)
    inverse_rms = lax.rsqrt(jnp.mean(squeezed * squeezed, axis=0, keepdims=True) + epsilon)
    return (squeezed * inverse_rms * gain[:, None]).astype(jnp.bfloat16)


def interact(joined):
    samples_now = joined.shape[1]
    values_f = joined.astype(jnp.float32).reshape(-1, CD, samples_now)
    gram = jnp.einsum("tck,uck->tuk", values_f, values_f, precision=lax.Precision.HIGHEST) / CD
    mixed = values_f + jnp.einsum("tuk,uck->tck", gram, values_f, precision=lax.Precision.HIGHEST)
    return mixed.reshape(-1, samples_now).astype(jnp.bfloat16)


def logit_terms(hidden_rows, hidden_bias, hidden_out, features):
    hidden = (
        jnp.dot(hidden_rows, features, preferred_element_type=jnp.float32)
        + hidden_bias.astype(jnp.float32)[:, None]
    )
    return jnp.sum(
        jax.nn.relu(hidden) * hidden_out.astype(jnp.float32)[:, None], axis=0, keepdims=True
    )


def on_device(
    pooled,
    feature_order,
    cross_weight,
    cross_bias,
    compress_weight,
    norm_gain,
    mlp_weight,
    mlp_bias,
    out_weight,
):
    micro_count = pooled.shape[0]
    arriving = [
        lax.all_to_all(pooled[batch], "rank", split_axis=1, concat_axis=0, tiled=True)
        for batch in range(micro_count)
    ]
    hidden_rows, hidden_bias, hidden_out = side_by_side(
        (mlp_weight, mlp_bias, out_weight), "tower", 0, 1
    )
    results = []
    for batch in range(micro_count):
        arrived = arriving[batch]
        samples_here = arrived.shape[1]
        first = jnp.take(arrived.reshape(-1, E, samples_here), feature_order[0], axis=0).reshape(
            -1, samples_here
        )
        compressed = tower_block(
            first, cross_weight[0], cross_bias[0], compress_weight[0], norm_gain[0]
        )
        tower_parts = lax.all_to_all(compressed, "tower", split_axis=1, concat_axis=0, tiled=True)
        mixed = interact(tower_parts)
        partial_value = logit_terms(
            hidden_rows, hidden_bias, hidden_out, lax.all_gather(mixed, "rank", axis=1, tiled=True)
        )
        logit_row = summed_on_arrival(partial_value, "rank", 1)
        results.append(logit_row)
    return jnp.stack(results)


def solution(mesh):
    return jax.shard_map(
        on_device,
        mesh=mesh,
        in_specs=(
            P(None, ("tower", "rank"), None),
            P("tower", None),
            P("tower", None, None, None),
            P("tower", None, None),
            P("tower", None, None),
            P("tower", None),
            P(("tower", "rank"), None),
            P(("tower", "rank")),
            P(("tower", "rank")),
        ),
        out_specs=P(None, "rank", "tower"),
        check_vma=False,
    )
```

profile of v0, /device:TPU:1, one launch (start us, length us, event | category | flops | bytes accessed | tf_op | source)
XLA Modules:
  0.0 249.7 jit_solution(15419998319595481402)
XLA Ops:
  6.5 0.0 copy-start
  6.5 1.3 fusion.58
  7.8 0.2 copy.84
  8.0 1.1 copy.64
  9.1 13.0 %all-to-all-start = ((bf16[16,32,512]{2,0,1:T(8,128)(2,1)}), bf16[16,32,512]{2,0,1:T(8,128)(2,1)S(1)}, u32[]{:S(2)}, u32[]{:S(2)}) async-start(bf16[16,32,512]{2,0,1:T(8,128)(2,1)} %copy.64), calls=%async_computation | async-start | bytes 1048576 | tf_op jit(solution)/shard_map/all_to_all | solution.py:79
  22.1 0.0 copy-start.8
  22.1 0.0 copy-start.2
  22.1 0.2 copy.86
  22.3 1.1 copy.72
  23.4 14.4 %all-to-all-done = bf16[16,32,512]{2,0,1:T(8,128)(2,1)S(1)} async-done(((bf16[16,32,512]{2,0,1:T(8,128)(2,1)}), bf16[16,32,512]{2,0,1:T(8,128)(2,1)S(1)}, u32[]{:S(2)}, u32[]{:S(2)}) %all-to-all-start) | async-done | bytes 524320 | tf_op jit(solution)/shard_map/all_to_all | solution.py:79
  37.8 5.5 %all-to-all-start.3 = ((bf16[16,32,512]{2,0,1:T(8,128)(2,1)}), bf16[16,32,512]{2,0,1:T(8,128)(2,1)S(1)}, u32[]{:S(2)}, u32[]{:S(2)}) async-start(bf16[16,32,512]{2,0,1:T(8,128)(2,1)} %copy.72), calls=%async_computation.3 | async-start | bytes 1048576 | tf_op jit(solution)/shard_map/all_to_all | solution.py:79
  43.3 0.0 all-gather.3.cloned.1.call-start
  43.3 0.0 copy-done.8
  43.4 0.0 copy-done.2
  43.4 0.6 gather_fusion
  44.0 15.0 %all-to-all-done.3 = bf16[16,32,512]{2,0,1:T(8,128)(2,1)S(1)} async-done(((bf16[16,32,512]{2,0,1:T(8,128)(2,1)}), bf16[16,32,512]{2,0,1:T(8,128)(2,1)S(1)}, u32[]{:S(2)}, u32[]{:S(2)}) %all-to-all-start.3) | async-done | bytes 524320 | tf_op jit(solution)/shard_map/all_to_all | solution.py:79
  59.0 0.6 gather_fusion.1
  59.6 0.2 broadcast_select_fusion.1
  59.7 0.2 copy.83
  59.9 0.2 copy.82
  60.2 0.0 copy-start.6
  60.2 1.7 fusion.11
  61.9 0.0 copy-done.6
  61.9 0.5 fusion.10
  62.4 1.3 fusion.14
  63.7 0.5 fusion.12
  64.3 0.0 copy-done
  64.3 0.9 copy-done.7
  65.1 2.0 multiply_reduce_fusion
  67.2 0.0 copy-start.5
  67.2 0.8 multiply_reduce_fusion.1
  68.0 0.0 copy-done.5
  68.0 0.2 multiply_convert_fusion.1
  68.2 0.0 copy-start.3
  68.2 0.0 copy-start.4
  68.3 0.0 copy-start.1
  68.3 18.7 %all_to_all.68 = bf16[128,16,32]{0,2,1:T(8,128)(2,1)S(1)} all-to-all(bf16[128,16,32]{0,2,1:T(8,128)(2,1)S(1)} %bitcast.175), channel_id=1, replica_groups=mesh['tower'=16,'rank'=32] {'tower'}, dimensions={1} | all-to-all | bytes 262144 | tf_op jit(solution)/shard_map/all_to_all | solution.py:95
  87.0 0.2 fusion.27
  87.2 0.4 fusion.28
  87.6 0.7 copy.99
  88.3 0.0 all-gather.3.cloned.1.call-update
  88.3 0.0 all-gather.5.cloned.1.call-start
  88.3 12.3 %all_to_all.69 = bf16[128,16,32]{0,2,1:T(8,128)(2,1)S(1)} all-to-all(bf16[128,16,32]{0,2,1:T(8,128)(2,1)S(1)} %bitcast.174), channel_id=1, replica_groups=mesh['tower'=16,'rank'=32] {'tower'}, dimensions={1} | all-to-all | bytes 262144 | tf_op jit(solution)/shard_map/all_to_all | solution.py:95
  100.7 0.2 fusion.25
  100.9 0.4 fusion.29
  101.3 0.7 copy.98
  101.9 0.0 all-gather.5.cloned.1.call-update
  102.0 0.0 copy-done.3
  102.0 0.1 copy.62
  102.1 0.1 copy.63
  102.2 0.1 concatenate.3
  102.3 38.0 %all_gather.9 = bf16[128,2050]{1,0:T(8,128)(2,1)S(1)} all-gather(bf16[8,2050]{1,0:T(8,128)(2,1)S(1)} %concatenate.3), channel_id=1, replica_groups=mesh['tower'=16,'rank'=32] {'tower'}, dimensions={0}, use_global_device_ids=true | all-gather | bytes 557600 | tf_op jit(solution)/shard_map/all_gather | solution.py:17
  140.3 0.2 convert_reduce_fusion.1
  140.4 11.5 %all-gather.3.cloned.1.call-done = bf16[2048,1024]{0,1:T(8,128)(2,1)} async-done(((bf16[2048,32]{0,1:T(8,128)(2,1)}), bf16[2048,1024]{0,1:T(8,128)(2,1)}) %all-gather.3.cloned.1.call-update) | async-done | bytes 4194320 | tf_op jit(solution)/shard_map/all_gather | solution.py:98
  152.0 3.7 %fusion.23 = f32[1024]{0:T(1024)S(1)} fusion(bf16[2048,1024]{0,1:T(8,128)(2,1)} %all-gather.3.cloned.1.call-done, bf16[128,2050]{1,0:T(8,128)(2,1)S(1)} %all_gather.9, f32[128]{0:T(128)S(1)} %get-tuple-element.7, f32[128]{0:T(128)S(1)} %get-tuple-element.6), kind=kOutput, calls=%fused_computation.41 | convolution fusion | flops 537394176 | bytes 4723712 | tf_op jit(solution)/shard_map/dot_general | solution.py:58
  155.7 0.7 transpose_reshape_broadcast_in_dim.6
  156.4 6.5 %all-to-all-start.2 = ((f32[32,1,32]{2,1,0:T(1,128)}), f32[32,1,32]{2,1,0:T(1,128)S(1)}, u32[]{:S(2)}, u32[]{:S(2)}) async-start(f32[32,1,32]{2,1,0:T(1,128)} %transpose_reshape_broadcast_in_dim.6), calls=%async_computation.2 | async-start | bytes 32768 | tf_op jit(solution)/shard_map/all_to_all | solution.py:30
  162.9 60.7 %all-gather.5.cloned.1.call-done = bf16[2048,1024]{0,1:T(8,128)(2,1)} async-done(((bf16[2048,32]{0,1:T(8,128)(2,1)}), bf16[2048,1024]{0,1:T(8,128)(2,1)}) %all-gather.5.cloned.1.call-update) | async-done | bytes 4194320 | tf_op jit(solution)/shard_map/all_gather | solution.py:98
  223.5 3.7 %fusion.22 = f32[1024]{0:T(1024)S(1)} fusion(bf16[2048,1024]{0,1:T(8,128)(2,1)} %all-gather.5.cloned.1.call-done, bf16[128,2050]{1,0:T(8,128)(2,1)S(1)} %all_gather.9, f32[128]{0:T(128)S(1)} %get-tuple-element.7, f32[128]{0:T(128)S(1)} %get-tuple-element.6), kind=kOutput, calls=%fused_computation.40 | convolution fusion | flops 537394176 | bytes 4723712 | tf_op jit(solution)/shard_map/dot_general | solution.py:58
  227.3 0.7 transpose_reshape_broadcast_in_dim.7
  228.0 0.0 all-to-all-done.2
  228.0 6.5 %all-to-all-start.5 = ((f32[32,1,32]{2,1,0:T(1,128)}), f32[32,1,32]{2,1,0:T(1,128)S(1)}, u32[]{:S(2)}, u32[]{:S(2)}) async-start(f32[32,1,32]{2,1,0:T(1,128)} %transpose_reshape_broadcast_in_dim.7), calls=%async_computation.5 | async-start | bytes 32768 | tf_op jit(solution)/shard_map/all_to_all | solution.py:30
  234.5 7.8 %all-to-all-done.5 = f32[32,1,32]{2,1,0:T(1,128)S(1)} async-done(((f32[32,1,32]{2,1,0:T(1,128)}), f32[32,1,32]{2,1,0:T(1,128)S(1)}, u32[]{:S(2)}, u32[]{:S(2)}) %all-to-all-start.5) | async-done | bytes 4128 | tf_op jit(solution)/shard_map/all_to_all | solution.py:30
  242.3 0.6 pad_maximum_fusion
  (10 shorter events, 0.1 us)
Async XLA Ops:
  6.5 57.7 %copy-start = (bf16[1,128,512]{2,1,0:T(8,128)(2,1)S(1)}, bf16[1,128,512]{2,1,0:T(8,128)(2,1)}, u32[]{:S(2)}) copy-start(bf16[1,128,512]{2,1,0:T(8,128)(2,1)} %param.15) | copy-start | bytes 393220
  9.1 28.7 %all-to-all-start = ((bf16[16,32,512]{2,0,1:T(8,128)(2,1)}), bf16[16,32,512]{2,0,1:T(8,128)(2,1)S(1)}, u32[]{:S(2)}, u32[]{:S(2)}) async-start(bf16[16,32,512]{2,0,1:T(8,128)(2,1)} %copy.64), calls=%async_computation | async-start | bytes 1048576 | tf_op jit(solution)/shard_map/all_to_all | solution.py:79
  22.1 21.2 %copy-start.8 = (s32[1,4]{1,0:T(1,128)S(1)}, s32[1,4]{1,0:T(1,128)}, u32[]{:S(2)}) copy-start(s32[1,4]{1,0:T(1,128)} %param.12) | copy-start | bytes 52
  22.1 21.3 %copy-start.2 = (f32[1,3,512]{2,0,1:T(1,128)S(1)}, f32[1,3,512]{2,0,1:T(1,128)}, u32[]{:S(2)}) copy-start(f32[1,3,512]{2,0,1:T(1,128)} %param.14) | copy-start | bytes 18436
  37.8 21.2 %all-to-all-start.3 = ((bf16[16,32,512]{2,0,1:T(8,128)(2,1)}), bf16[16,32,512]{2,0,1:T(8,128)(2,1)S(1)}, u32[]{:S(2)}, u32[]{:S(2)}) async-start(bf16[16,32,512]{2,0,1:T(8,128)(2,1)} %copy.72), calls=%async_computation.3 | async-start | bytes 1048576 | tf_op jit(solution)/shard_map/all_to_all | solution.py:79
  43.3 108.7 %all-gather.3.cloned.1.call-start = ((), (), s32[]{:S(2)}) async-start(), calls=%async_computation.6 | async-start | bytes 4325376 | tf_op jit(solution)/shard_map/all_gather | solution.py:98
  60.2 1.7 copy-start.6
  63.7 1.4 copy-start.7
  67.2 0.8 copy-start.5
  68.2 33.7 %copy-start.3 = (bf16[8]{0:T(256)(128)(2,1)S(1)}, bf16[8]{0:T(256)(128)(2,1)}, u32[]{:S(2)}) copy-start(bf16[8]{0:T(256)(128)(2,1)} %param.18) | copy-start | bytes 52
  68.2 33.8 %copy-start.4 = (bf16[8]{0:T(256)(128)(2,1)S(1)}, bf16[8]{0:T(256)(128)(2,1)}, u32[]{:S(2)}) copy-start(bf16[8]{0:T(256)(128)(2,1)} %param.19) | copy-start | bytes 52
  68.3 33.9 %copy-start.1 = (bf16[8,2048]{1,0:T(8,128)(2,1)S(1)}, bf16[8,2048]{1,0:T(8,128)(2,1)}, u32[]{:S(2)}) copy-start(bf16[8,2048]{1,0:T(8,128)(2,1)} %param.17) | copy-start | bytes 98308
  88.3 135.2 %all-gather.5.cloned.1.call-start = ((), (), s32[]{:S(2)}) async-start(), calls=%async_computation.7 | async-start | bytes 4325376 | tf_op jit(solution)/shard_map/all_gather | solution.py:98
  156.4 71.6 %all-to-all-start.2 = ((f32[32,1,32]{2,1,0:T(1,128)}), f32[32,1,32]{2,1,0:T(1,128)S(1)}, u32[]{:S(2)}, u32[]{:S(2)}) async-start(f32[32,1,32]{2,1,0:T(1,128)} %transpose_reshape_broadcast_in_dim.6), calls=%async_computation.2 | async-start | bytes 32768 | tf_op jit(solution)/shard_map/all_to_all | solution.py:30
  228.0 14.3 %all-to-all-start.5 = ((f32[32,1,32]{2,1,0:T(1,128)}), f32[32,1,32]{2,1,0:T(1,128)S(1)}, u32[]{:S(2)}, u32[]{:S(2)}) async-start(f32[32,1,32]{2,1,0:T(1,128)} %transpose_reshape_broadcast_in_dim.7), calls=%async_computation.5 | async-start | bytes 32768 | tf_op jit(solution)/shard_map/all_to_all | solution.py:30
Sparse Core Ops, SparseCore 0:
  88.4 63.5 all-gather.2
  154.1 69.3 all-gather.4
where the time goes:
time: 250 us
  waiting for transfers between devices  109 us (44%)
  blocking collectives  69 us (28%)
  starting transfers between devices  31.5 us (13%)
  matrix products  15.5 us (6%)
  between operations  13.7 us (5%)
  local copies, waits for them, and re-layouts  9.29 us (4%)
    all_gather x2, waiting for transfers between devices, on_device(): lax.all_gather(mixed, 'rank', axis=1, tiled=True)  72.2 us
    all_gather x1, blocking collectives, side_by_side(): whole = lax.all_gather(both, axis, axis=dim, tiled=True)  38 us
    all_to_all x2, blocking collectives, on_device(): lax.all_to_all(compressed, 'tower', split_axis=1, concat_axis=0, tiled=True)  31 us
    all_to_all x2, waiting for transfers between devices, on_device(): lax.all_to_all(pooled[batch], 'rank', split_axis=1, concat_axis=0, tiled=...  29.4 us
    all_to_all x2, starting transfers between devices, on_device(): lax.all_to_all(pooled[batch], 'rank', split_axis=1, concat_axis=0, tiled=...  18.4 us
    all_to_all x2, starting transfers between devices, summed_on_arrival(): lax.all_to_all(parts, axis, split_axis=0, concat_axis=0, tiled=True)  13 us
    all_to_all x2, waiting for transfers between devices, summed_on_arrival(): lax.all_to_all(parts, axis, split_axis=0, concat_axis=0, tiled=True)  7.8 us
    dot_general x2, matrix products, logit_terms(): jnp.dot(hidden_rows, features, preferred_element_type=jnp.float32)  7.43 us
  transfers between devices with their start and end apart: 6, of which 5 were waited for; matrix products, arithmetic and copies ran while one was open for 5% of the time, Pallas kernels for 0%

commit v1 on v0

--- a/solution.py
+++ b/solution.py
@@ -94,9 +94,20 @@
         )
         tower_parts = lax.all_to_all(compressed, "tower", split_axis=1, concat_axis=0, tiled=True)
         mixed = interact(tower_parts)
-        partial_value = logit_terms(
-            hidden_rows, hidden_bias, hidden_out, lax.all_gather(mixed, "rank", axis=1, tiled=True)
-        )
+
+        def _connect_vector(chunk):
+            o_now = jnp.concatenate(
+                lax.all_to_all(
+                    jnp.stack([chunk] * lax.psum(1, "rank")),
+                    axis_name="rank",
+                    split_axis=0,
+                    concat_axis=0,
+                ),
+                1,
+            )
+            return o_now
+
+        partial_value = logit_terms(hidden_rows, hidden_bias, hidden_out, _connect_vector(mixed))
         logit_row = summed_on_arrival(partial_value, "rank", 1)
         results.append(logit_row)
     return jnp.stack(results)

time: 250 us -> 364 us (1.46)
  blocking collectives: 69 us -> 127 us
  waiting for transfers between devices: 109 us -> 152 us
  starting transfers between devices: 31.5 us -> 53.3 us
  between operations: 13.7 us -> 0.31 us
  local copies, waits for them, and re-layouts: 9.29 us -> 13 us
    all_to_all x0 -> x3, waiting for transfers between devices: none -> 111 us  [the longest x2 102 us: _connect_vector(): lax.all_to_all(jnp.stack([chunk] * lax.psum(1, 'rank')), axis_name='rank'...]
    all_gather x2 -> x0, waiting for transfers between devices: 72.2 us -> none  [on_device(): lax.all_gather(mixed, 'rank', axis=1, tiled=True)]
    all_gather x1, blocking collectives: 38 us -> 108 us  [side_by_side(): whole = lax.all_gather(both, axis, axis=dim, tiled=True)]
    all_to_all x0 -> x3, starting transfers between devices: none -> 16.5 us  [the longest x2 13 us: _connect_vector(): lax.all_to_all(jnp.stack([chunk] * lax.psum(1, 'rank')), axis_name='rank'...]
    all_to_all x2 -> x1, blocking collectives: 31 us -> 18.6 us  [on_device(): lax.all_to_all(compressed, 'tower', split_axis=1, concat_axis=0, tiled=True)]
    all_to_all x2, starting transfers between devices: 13 us -> 18.3 us  [summed_on_arrival(): lax.all_to_all(parts, axis, split_axis=0, concat_axis=0, tiled=True)]
    another operation x0 -> x2, local copies, waits for them, and re-layouts: none -> 5 us  [_connect_vector(): jnp.stack([chunk] * lax.psum(1, 'rank'))]
  transfers between devices with their start and end apart: 6 -> 7, of which waited for: 5 -> 6; matrix products, arithmetic and copies ran while one was open for 5% -> 3% of each run, Pallas kernels for 0% -> 0%
where the time goes in v1:
time: 364 us; the launch traced here: 363 us
  waiting for transfers between devices  152 us (42%)
  blocking collectives  127 us (35%)
  starting transfers between devices  53.3 us (15%)
  matrix products  15.6 us (4%)
  local copies, waits for them, and re-layouts  13 us (4%)
    all_gather x1, blocking collectives, side_by_side(): whole = lax.all_gather(both, axis, axis=dim, tiled=True)  108 us
    all_to_all x2, waiting for transfers between devices, _connect_vector(): lax.all_to_all(jnp.stack([chunk] * lax.psum(1, 'rank')), axis_name='rank'...  102 us
    all_to_all x2, waiting for transfers between devices, on_device(): lax.all_to_all(pooled[batch], 'rank', split_axis=1, concat_axis=0, tiled=...  29.5 us
    all_to_all x1, blocking collectives, on_device(): lax.all_to_all(compressed, 'tower', split_axis=1, concat_axis=0, tiled=True)  18.6 us
    all_to_all x2, starting transfers between devices, on_device(): lax.all_to_all(pooled[batch], 'rank', split_axis=1, concat_axis=0, tiled=...  18.4 us
    all_to_all x2, starting transfers between devices, summed_on_arrival(): lax.all_to_all(parts, axis, split_axis=0, concat_axis=0, tiled=True)  18.3 us
    all_to_all x2, starting transfers between devices, _connect_vector(): lax.all_to_all(jnp.stack([chunk] * lax.psum(1, 'rank')), axis_name='rank'...  13 us
    all_to_all x2, waiting for transfers between devices, summed_on_arrival(): lax.all_to_all(parts, axis, split_axis=0, concat_axis=0, tiled=True)  11.2 us
  transfers between devices with their start and end apart: 7, of which 6 were waited for; matrix products, arithmetic and copies ran while one was open for 3% of the time, Pallas kernels for 0%

profile of v1, /device:TPU:1, one launch (start us, length us, event | category | flops | bytes accessed | tf_op | source)
XLA Modules:
  0.0 363.1 jit_solution(4905447913745403523)
XLA Ops:
  0.0 0.0 copy-start
  0.0 1.3 fusion.58
  1.3 0.2 copy.86
  1.5 1.1 copy.66
  2.6 13.0 %all-to-all-start = ((bf16[16,32,512]{2,0,1:T(8,128)(2,1)}), bf16[16,32,512]{2,0,1:T(8,128)(2,1)S(1)}, u32[]{:S(2)}, u32[]{:S(2)}) async-start(bf16[16,32,512]{2,0,1:T(8,128)(2,1)} %copy.66), calls=%async_computation | async-start | bytes 1048576 | tf_op jit(solution)/shard_map/all_to_all | solution.py:79
  15.6 0.0 copy-start.8
  15.6 0.0 copy-start.2
  15.6 0.2 copy.88
  15.7 1.1 copy.74
  16.8 14.4 %all-to-all-done = bf16[16,32,512]{2,0,1:T(8,128)(2,1)S(1)} async-done(((bf16[16,32,512]{2,0,1:T(8,128)(2,1)}), bf16[16,32,512]{2,0,1:T(8,128)(2,1)S(1)}, u32[]{:S(2)}, u32[]{:S(2)}) %all-to-all-start) | async-done | bytes 524320 | tf_op jit(solution)/shard_map/all_to_all | solution.py:79
  31.3 5.5 %all-to-all-start.4 = ((bf16[16,32,512]{2,0,1:T(8,128)(2,1)}), bf16[16,32,512]{2,0,1:T(8,128)(2,1)S(1)}, u32[]{:S(2)}, u32[]{:S(2)}) async-start(bf16[16,32,512]{2,0,1:T(8,128)(2,1)} %copy.74), calls=%async_computation.4 | async-start | bytes 1048576 | tf_op jit(solution)/shard_map/all_to_all | solution.py:79
  36.7 0.0 copy-done.8
  36.8 0.0 copy-done.2
  36.8 0.6 gather_fusion
  37.4 15.1 %all-to-all-done.4 = bf16[16,32,512]{2,0,1:T(8,128)(2,1)S(1)} async-done(((bf16[16,32,512]{2,0,1:T(8,128)(2,1)}), bf16[16,32,512]{2,0,1:T(8,128)(2,1)S(1)}, u32[]{:S(2)}, u32[]{:S(2)}) %all-to-all-start.4) | async-done | bytes 524320 | tf_op jit(solution)/shard_map/all_to_all | solution.py:79
  52.4 0.6 gather_fusion.1
  53.0 0.2 broadcast_select_fusion.1
  53.2 0.2 copy.85
  53.4 0.2 copy.84
  53.6 0.0 copy-start.6
  53.6 1.7 fusion.11
  55.3 0.0 copy-done.6
  55.3 0.5 fusion.10
  55.9 1.3 fusion.14
  57.2 0.0 copy-start.7
  57.2 0.5 fusion.12
  57.7 0.0 copy-done
  57.7 0.9 copy-done.7
  58.6 2.0 multiply_reduce_fusion
  60.6 0.0 copy-start.5
  60.7 0.8 multiply_reduce_fusion.1
  61.5 0.0 copy-done.5
  61.5 0.8 multiply_convert_fusion.1
  62.3 18.6 %all_to_all.78 = bf16[128,16,32]{0,2,1:T(8,128)(2,1)S(1)} all-to-all(bf16[128,16,32]{0,2,1:T(8,128)(2,1)S(1)} %bitcast.180), channel_id=1, replica_groups=mesh['tower'=16,'rank'=32] {'tower'}, dimensions={1} | all-to-all | bytes 262144 | tf_op jit(solution)/shard_map/all_to_all | solution.py:95
  81.0 3.5 all-to-all-start.5
  84.5 0.2 fusion.27
  84.7 0.4 fusion.28
  85.1 9.0 %all-to-all-done.5 = bf16[128,16,32]{0,2,1:T(8,128)(2,1)S(1)} async-done(((bf16[128,16,32]{0,2,1:T(8,128)(2,1)}), bf16[128,16,32]{0,2,1:T(8,128)(2,1)S(1)}, u32[]{:S(2)}, u32[]{:S(2)}) %all-to-all-start.5) | async-done | bytes 131104 | tf_op jit(solution)/shard_map/all_to_all | solution.py:95
  94.1 2.5 stack.10
  96.7 7.4 %all-to-all-start.2 = ((bf16[32,2048,32]{1,2,0:T(8,128)(2,1)}), bf16[32,2048,32]{1,2,0:T(8,128)(2,1)}, u32[]{:S(2)}, u32[]{:S(2)}) async-start(bf16[32,2048,32]{1,2,0:T(8,128)(2,1)} %stack.10), calls=%async_computation.2 | async-start | bytes 8388608 | tf_op jit(solution)/shard_map/all_to_all | solution.py:100
  104.1 0.2 fusion.25
  104.3 0.4 fusion.29
  104.7 102.4 %all-to-all-done.2 = bf16[32,2048,32]{1,2,0:T(8,128)(2,1)} async-done(((bf16[32,2048,32]{1,2,0:T(8,128)(2,1)}), bf16[32,2048,32]{1,2,0:T(8,128)(2,1)}, u32[]{:S(2)}, u32[]{:S(2)}) %all-to-all-start.2) | async-done | bytes 4194336 | tf_op jit(solution)/shard_map/all_to_all | solution.py:100
  207.1 2.5 stack.12
  209.6 0.0 copy-start.3
  209.6 5.6 %all-to-all-start.6 = ((bf16[32,2048,32]{1,2,0:T(8,128)(2,1)}), bf16[32,2048,32]{1,2,0:T(8,128)(2,1)}, u32[]{:S(2)}, u32[]{:S(2)}) async-start(bf16[32,2048,32]{1,2,0:T(8,128)(2,1)} %stack.12), calls=%async_computation.6 | async-start | bytes 8388608 | tf_op jit(solution)/shard_map/all_to_all | solution.py:100
  215.3 0.0 copy-done.3
  215.3 0.1 copy.64
  215.4 0.0 copy-done.4
  215.4 0.1 copy.65
  215.5 0.0 copy-done.1
  215.5 0.1 concatenate.3
  215.6 108.5 %all_gather.3 = bf16[128,2050]{1,0:T(8,128)(2,1)S(1)} all-gather(bf16[8,2050]{1,0:T(8,128)(2,1)S(1)} %concatenate.3), channel_id=1, replica_groups=mesh['tower'=16,'rank'=32] {'tower'}, dimensions={0}, use_global_device_ids=true | all-gather | bytes 557600 | tf_op jit(solution)/shard_map/all_gather | solution.py:17
  324.0 0.2 convert_reduce_fusion.1
  324.2 3.7 %fusion.23 = f32[1024]{0:T(1024)S(1)} fusion(bf16[2048,1024]{0,1:T(8,128)(2,1)} %bitcast.23, bf16[128,2050]{1,0:T(8,128)(2,1)S(1)} %all_gather.3, f32[128]{0:T(128)S(1)} %get-tuple-element.7, f32[128]{0:T(128)S(1)} %get-tuple-element.6), kind=kOutput, calls=%fused_computation.41 | convolution fusion | flops 537394176 | bytes 4723712 | tf_op jit(solution)/shard_map/dot_general | solution.py:58
  327.9 0.7 transpose_reshape_broadcast_in_dim.6
  328.6 0.0 all-to-all-done.6
  328.6 13.4 %all-to-all-start.3 = ((f32[32,1,32]{2,1,0:T(1,128)}), f32[32,1,32]{2,1,0:T(1,128)S(1)}, u32[]{:S(2)}, u32[]{:S(2)}) async-start(f32[32,1,32]{2,1,0:T(1,128)} %transpose_reshape_broadcast_in_dim.6), calls=%async_computation.3 | async-start | bytes 32768 | tf_op jit(solution)/shard_map/all_to_all | solution.py:30
  342.0 3.7 %fusion.22 = f32[1024]{0:T(1024)S(1)} fusion(bf16[2048,1024]{0,1:T(8,128)(2,1)} %bitcast.38, bf16[128,2050]{1,0:T(8,128)(2,1)S(1)} %all_gather.3, f32[128]{0:T(128)S(1)} %get-tuple-element.7, f32[128]{0:T(128)S(1)} %get-tuple-element.6), kind=kOutput, calls=%fused_computation.40 | convolution fusion | flops 537394176 | bytes 4723712 | tf_op jit(solution)/shard_map/dot_general | solution.py:58
  345.7 0.7 transpose_reshape_broadcast_in_dim.7
  346.4 3.4 all-to-all-done.3
  349.8 4.9 %all-to-all-start.7 = ((f32[32,1,32]{2,1,0:T(1,128)}), f32[32,1,32]{2,1,0:T(1,128)S(1)}, u32[]{:S(2)}, u32[]{:S(2)}) async-start(f32[32,1,32]{2,1,0:T(1,128)} %transpose_reshape_broadcast_in_dim.7), calls=%async_computation.7 | async-start | bytes 32768 | tf_op jit(solution)/shard_map/all_to_all | solution.py:30
  354.8 7.8 %all-to-all-done.7 = f32[32,1,32]{2,1,0:T(1,128)S(1)} async-done(((f32[32,1,32]{2,1,0:T(1,128)}), f32[32,1,32]{2,1,0:T(1,128)S(1)}, u32[]{:S(2)}, u32[]{:S(2)}) %all-to-all-start.7) | async-done | bytes 4128 | tf_op jit(solution)/shard_map/all_to_all | solution.py:30
  362.6 0.6 pad_maximum_fusion
  (11 shorter events, 0.2 us)
Async XLA Ops:
  0.0 57.7 %copy-start = (bf16[1,128,512]{2,1,0:T(8,128)(2,1)S(1)}, bf16[1,128,512]{2,1,0:T(8,128)(2,1)}, u32[]{:S(2)}) copy-start(bf16[1,128,512]{2,1,0:T(8,128)(2,1)} %param.15) | copy-start | bytes 393220
  2.6 28.7 %all-to-all-start = ((bf16[16,32,512]{2,0,1:T(8,128)(2,1)}), bf16[16,32,512]{2,0,1:T(8,128)(2,1)S(1)}, u32[]{:S(2)}, u32[]{:S(2)}) async-start(bf16[16,32,512]{2,0,1:T(8,128)(2,1)} %copy.66), calls=%async_computation | async-start | bytes 1048576 | tf_op jit(solution)/shard_map/all_to_all | solution.py:79
  15.6 21.2 %copy-start.8 = (s32[1,4]{1,0:T(1,128)S(1)}, s32[1,4]{1,0:T(1,128)}, u32[]{:S(2)}) copy-start(s32[1,4]{1,0:T(1,128)} %param.12) | copy-start | bytes 52
  15.6 21.2 %copy-start.2 = (f32[1,3,512]{2,0,1:T(1,128)S(1)}, f32[1,3,512]{2,0,1:T(1,128)}, u32[]{:S(2)}) copy-start(f32[1,3,512]{2,0,1:T(1,128)} %param.14) | copy-start | bytes 18436
  31.3 21.2 %all-to-all-start.4 = ((bf16[16,32,512]{2,0,1:T(8,128)(2,1)}), bf16[16,32,512]{2,0,1:T(8,128)(2,1)S(1)}, u32[]{:S(2)}, u32[]{:S(2)}) async-start(bf16[16,32,512]{2,0,1:T(8,128)(2,1)} %copy.74), calls=%async_computation.4 | async-start | bytes 1048576 | tf_op jit(solution)/shard_map/all_to_all | solution.py:79
  53.6 1.7 copy-start.6
  57.2 1.4 copy-start.7
  60.6 0.8 copy-start.5
  81.0 13.2 %all-to-all-start.5 = ((bf16[128,16,32]{0,2,1:T(8,128)(2,1)}), bf16[128,16,32]{0,2,1:T(8,128)(2,1)S(1)}, u32[]{:S(2)}, u32[]{:S(2)}) async-start(bf16[128,16,32]{0,2,1:T(8,128)(2,1)} %bitcast.33), calls=%async_computation.5 | async-start | bytes 262144 | tf_op jit(solution)/shard_map/all_to_all | solution.py:95
  96.7 110.5 %all-to-all-start.2 = ((bf16[32,2048,32]{1,2,0:T(8,128)(2,1)}), bf16[32,2048,32]{1,2,0:T(8,128)(2,1)}, u32[]{:S(2)}, u32[]{:S(2)}) async-start(bf16[32,2048,32]{1,2,0:T(8,128)(2,1)} %stack.10), calls=%async_computation.2 | async-start | bytes 8388608 | tf_op jit(solution)/shard_map/all_to_all | solution.py:100
  209.6 5.6 %copy-start.3 = (bf16[8]{0:T(256)(128)(2,1)S(1)}, bf16[8]{0:T(256)(128)(2,1)}, u32[]{:S(2)}) copy-start(bf16[8]{0:T(256)(128)(2,1)} %param.18) | copy-start | bytes 52
  209.6 5.7 %copy-start.4 = (bf16[8]{0:T(256)(128)(2,1)S(1)}, bf16[8]{0:T(256)(128)(2,1)}, u32[]{:S(2)}) copy-start(bf16[8]{0:T(256)(128)(2,1)} %param.19) | copy-start | bytes 52
  209.6 5.8 %copy-start.1 = (bf16[8,2048]{1,0:T(8,128)(2,1)S(1)}, bf16[8,2048]{1,0:T(8,128)(2,1)}, u32[]{:S(2)}) copy-start(bf16[8,2048]{1,0:T(8,128)(2,1)} %param.17) | copy-start | bytes 98308
  209.6 119.0 %all-to-all-start.6 = ((bf16[32,2048,32]{1,2,0:T(8,128)(2,1)}), bf16[32,2048,32]{1,2,0:T(8,128)(2,1)}, u32[]{:S(2)}, u32[]{:S(2)}) async-start(bf16[32,2048,32]{1,2,0:T(8,128)(2,1)} %stack.12), calls=%async_computation.6 | async-start | bytes 8388608 | tf_op jit(solution)/shard_map/all_to_all | solution.py:100
  328.6 21.2 %all-to-all-start.3 = ((f32[32,1,32]{2,1,0:T(1,128)}), f32[32,1,32]{2,1,0:T(1,128)S(1)}, u32[]{:S(2)}, u32[]{:S(2)}) async-start(f32[32,1,32]{2,1,0:T(1,128)} %transpose_reshape_broadcast_in_dim.6), calls=%async_computation.3 | async-start | bytes 32768 | tf_op jit(solution)/shard_map/all_to_all | solution.py:30
  349.8 12.7 %all-to-all-start.7 = ((f32[32,1,32]{2,1,0:T(1,128)}), f32[32,1,32]{2,1,0:T(1,128)S(1)}, u32[]{:S(2)}, u32[]{:S(2)}) async-start(f32[32,1,32]{2,1,0:T(1,128)} %transpose_reshape_broadcast_in_dim.7), calls=%async_computation.7 | async-start | bytes 32768 | tf_op jit(solution)/shard_map/all_to_all | solution.py:30
